TPU v7x, 32 devices: a whole 2x2x4 slice. The times are simulated.
32 devices in a mesh: groups: 2 (over y), lat: 16 (over z, x, core).
Axes of the slice: x: 2, y: 2, z: 4, core: 2. Of those that a mesh axis runs over, the one named last changes fastest.
Arguments:
- grid_state: bfloat16 [8192, 227], P(('groups', 'lat')), parts along dimension 0, may hold values from -6 to 6
- mesh_embed: bfloat16 [1024, 512], P(('groups', 'lat')), parts along dimension 0, may hold values from -6 to 6
- g2m_owner: int32 [8192, 2], P(('groups', 'lat')), parts along dimension 0, may hold values from 0 to 15, all different within a row; in each aligned block of 256 rows (0 to 255, 256 to 511, ...) at most 64 rows name the same one
- g2m_node: int32 [8192, 2], P(('groups', 'lat')), parts along dimension 0, may hold values from 0 to 31
- mm_owner: int32 [1024, 8], P(('groups', 'lat')), parts along dimension 0, may hold values from 0 to 15, all different within a row; in each aligned block of 32 rows (0 to 31, 32 to 63, ...) at most 32 rows name the same one
- mm_node: int32 [1024, 8], P(('groups', 'lat')), parts along dimension 0, may hold values from 0 to 31
- m2g_owner: int32 [8192, 3], P(('groups', 'lat')), parts along dimension 0, may hold values from 0 to 15, all different within a row; in each aligned block of 256 rows (0 to 255, 256 to 511, ...) at most 96 rows name the same one
- m2g_node: int32 [8192, 3], P(('groups', 'lat')), parts along dimension 0, may hold values from 0 to 31
- embed_in: bfloat16 [227, 512], replicated, may hold values from -0.375 to 0.375
- embed_out: bfloat16 [512, 512], replicated, may hold values from -0.25 to 0.25
- g2m_in: bfloat16 [1024, 512], replicated, may hold values from -0.1875 to 0.1875
- g2m_out: bfloat16 [512, 512], replicated, may hold values from -0.25 to 0.25
- mesh_in: bfloat16 [1024, 512], replicated, may hold values from -0.1875 to 0.1875
- mesh_out: bfloat16 [512, 512], replicated, may hold values from -0.25 to 0.25
- edge_in: bfloat16 [1024, 512], replicated, may hold values from -0.1875 to 0.1875
- edge_out: bfloat16 [512, 512], replicated, may hold values from -0.25 to 0.25
- node_in: bfloat16 [1024, 512], replicated, may hold values from -0.1875 to 0.1875
- node_out: bfloat16 [512, 512], replicated, may hold values from -0.25 to 0.25
- m2g_in: bfloat16 [1024, 512], replicated, may hold values from -0.1875 to 0.1875
- m2g_out: bfloat16 [512, 512], replicated, may hold values from -0.25 to 0.25
- grid_in: bfloat16 [1024, 512], replicated, may hold values from -0.1875 to 0.1875
- grid_out: bfloat16 [512, 227], replicated, may hold values from -0.25 to 0.25
Outputs:
- increment: bfloat16 [8192, 227], P(('groups', 'lat')), parts along dimension 0
There are 2 independent parts, one for each index of `groups`. A program takes and returns all parts, laid end to end along the dimension named above; an argument that names none is the same for every part. Nothing has to cross between parts.
Inputs may be any that keep to these rules, and one draw needn't show every extreme that they name: `g2m_owner`: each row names 2 different owners; among the 256 rows of one device no owner is named by more than 64 rows, and some owner reaches it. `mm_owner`: each row names 8 different owners; among the 32 rows of one device no owner is named by more than 32 rows, and some owner reaches it. `m2g_owner`: each row names 3 different owners; among the 256 rows of one device no owner is named by more than 96 rows, and some owner reaches it.
All inputs are finite; a program needn't handle non-finite values.
Results may differ from a plain program's by a relative error of at most 0.015.
Values may be sent and summed in bfloat16 or wider, within the bound.
A program may use at most 64 MiB of HBM per device.

v0:
```python
import jax
import jax.numpy as jnp
from jax import lax
from jax.sharding import PartitionSpec as P


def layer_norm(values):
    center = values - jnp.mean(values, axis=-1, keepdims=True)
    spread = jnp.mean(center * center, axis=-1, keepdims=True)
    return center * lax.rsqrt(spread + 1e-05)


def mlp_tail(preact, w_out):
    hidden = jax.nn.silu(preact).astype(jnp.bfloat16)
    return layer_norm(jnp.dot(hidden, w_out, preferred_element_type=jnp.float32))


def node_mlp(left, right, w_in, w_out):
    joined = jnp.concatenate([left, right], axis=1)
    return mlp_tail(jnp.dot(joined, w_in, preferred_element_type=jnp.float32), w_out)


def slot_index(owners, capacity):
    total = owners.shape[0]
    position = jnp.arange(total, dtype=jnp.int32)
    matches = (owners[:, None] == owners[None, :]) & (position[None, :] < position[:, None])
    return owners * capacity + jnp.sum(matches.astype(jnp.int32), axis=1)


def capacity_of(edge_count, peer_count):
    return max(2, (2 * edge_count + peer_count - 1) // peer_count)


def body(
    grid_state,
    mesh_embed,
    g2m_owner,
    g2m_node,
    mm_owner,
    mm_node,
    m2g_owner,
    m2g_node,
    embed_in,
    embed_out,
    g2m_in,
    g2m_out,
    mesh_in,
    mesh_out,
    edge_in,
    edge_out,
    node_in,
    node_out,
    m2g_in,
    m2g_out,
    grid_in,
    grid_out,
):
    peer_count = lax.axis_size("lat")
    latent_width = embed_out.shape[1]
    grid_rows = grid_state.shape[0]
    mesh_rows = mesh_embed.shape[0]
    grid_latent = mlp_tail(
        jnp.dot(grid_state, embed_in, preferred_element_type=jnp.float32), embed_out
    ).astype(jnp.bfloat16)
    fan_grid = g2m_owner.shape[1]
    cap_grid = capacity_of(grid_rows * fan_grid, peer_count)
    grid_slots = slot_index(g2m_owner.reshape(-1), cap_grid)
    outgoing = jnp.repeat(grid_latent, fan_grid, axis=0)
    send_rows = (
        jnp.zeros((peer_count * cap_grid, latent_width), jnp.bfloat16).at[grid_slots].set(outgoing)
    )
    send_rows = send_rows.reshape(peer_count, cap_grid, latent_width)
    send_nodes = (
        jnp.full((peer_count * cap_grid,), mesh_rows, jnp.int32)
        .at[grid_slots]
        .set(g2m_node.reshape(-1))
    )
    send_nodes = send_nodes.reshape(peer_count, cap_grid)
    receiver_part = jnp.dot(mesh_embed, g2m_in[latent_width:], preferred_element_type=jnp.float32)
    receiver_padded = jnp.concatenate(
        [receiver_part, jnp.zeros((1, latent_width), jnp.float32)], axis=0
    )
    slot_rows = lax.all_to_all(send_rows, "lat", split_axis=0, concat_axis=0, tiled=True)
    slot_nodes = lax.all_to_all(send_nodes, "lat", split_axis=0, concat_axis=0, tiled=True)
    preact = jnp.einsum(
        "pch,hk->pck", slot_rows, g2m_in[:latent_width], preferred_element_type=jnp.float32
    )
    preact = preact + receiver_padded[slot_nodes]
    hidden = jax.nn.silu(preact).astype(jnp.bfloat16)
    result = jnp.einsum("pch,hk->pck", hidden, g2m_out, preferred_element_type=jnp.float32)
    arrived = layer_norm(result).astype(jnp.bfloat16)
    one_hot = (
        slot_nodes.reshape(-1)[:, None] == jnp.arange(mesh_rows, dtype=jnp.int32)[None, :]
    ).astype(jnp.bfloat16)
    g2m_sum = jnp.einsum(
        "rm,rh->mh", one_hot, arrived.reshape(-1, latent_width), preferred_element_type=jnp.float32
    ).astype(jnp.bfloat16)
    mesh_latent = (
        mesh_embed.astype(jnp.float32) + node_mlp(mesh_embed, g2m_sum, mesh_in, mesh_out)
    ).astype(jnp.bfloat16)
    fan_mesh = mm_owner.shape[1]
    every_mesh = lax.all_gather(mesh_latent, "lat", axis=0, tiled=True)
    mesh_senders = every_mesh[(mm_owner * mesh_rows + mm_node).reshape(-1)]
    receiver_mesh = jnp.dot(mesh_latent, edge_in[latent_width:], preferred_element_type=jnp.float32)
    preact = jnp.dot(mesh_senders, edge_in[:latent_width], preferred_element_type=jnp.float32)
    preact = preact + jnp.repeat(receiver_mesh, fan_mesh, axis=0)
    mesh_message = mlp_tail(preact, edge_out).astype(jnp.bfloat16)
    mesh_sum = jnp.sum(
        mesh_message.astype(jnp.float32).reshape(mesh_rows, fan_mesh, latent_width), axis=1
    ).astype(jnp.bfloat16)
    mesh_final = (
        mesh_latent.astype(jnp.float32) + node_mlp(mesh_latent, mesh_sum, node_in, node_out)
    ).astype(jnp.bfloat16)
    fan_down = m2g_owner.shape[1]
    every_final = lax.all_gather(mesh_final, "lat", axis=0, tiled=True)
    grid_senders = every_final[(m2g_owner * mesh_rows + m2g_node).reshape(-1)]
    receiver_grid = jnp.dot(grid_latent, m2g_in[latent_width:], preferred_element_type=jnp.float32)
    preact = jnp.dot(grid_senders, m2g_in[:latent_width], preferred_element_type=jnp.float32)
    preact = preact + jnp.repeat(receiver_grid, fan_down, axis=0)
    down_message = mlp_tail(preact, m2g_out).astype(jnp.bfloat16)
    down_sum = jnp.sum(
        down_message.astype(jnp.float32).reshape(grid_rows, fan_down, latent_width), axis=1
    ).astype(jnp.bfloat16)
    joined = jnp.concatenate([grid_latent, down_sum], axis=1)
    grid_hidden = jax.nn.silu(jnp.dot(joined, grid_in, preferred_element_type=jnp.float32)).astype(
        jnp.bfloat16
    )
    return jnp.dot(grid_hidden, grid_out, preferred_element_type=jnp.float32).astype(jnp.bfloat16)


def solution(mesh):
    in_specs = (
        P(("groups", "lat"), None),
        P(("groups", "lat"), None),
        P(("groups", "lat"), None),
        P(("groups", "lat"), None),
        P(("groups", "lat"), None),
        P(("groups", "lat"), None),
        P(("groups", "lat"), None),
        P(("groups", "lat"), None),
        P(),
        P(),
        P(),
        P(),
        P(),
        P(),
        P(),
        P(),
        P(),
        P(),
        P(),
        P(),
        P(),
        P(),
    )
    out_specs = P(("groups", "lat"), None)
    return jax.shard_map(body, mesh=mesh, in_specs=in_specs, out_specs=out_specs, check_vma=False)
```

profile of v0, /device:TPU:0, one launch (start us, length us, event | category | flops | bytes accessed | tf_op | source)
XLA Modules:
  0.0 114.6 jit_solution(2390316124992250565)
XLA Ops:
  0.0 0.9 copy.29
  0.9 0.7 broadcast_multiply_fusion.2
  2.3 0.8 copy.30
  3.3 2.4 %scatter_custom_fusion = s32[1024]{0:T(1024)S(1)} fusion(s32[512]{0:T(512)S(1)} %bitcast.55, s32[512]{0:T(512)S(1)} %reshape.269, s32[]{:T(128)} %constant.23.clone.1), kind=kCustom, calls=%fused_computation.87 | custom fusion | bytes 4100 | tf_op jit(solution)/shard_map/scatter | solution.py:76
  5.7 0.7 all_to_all.11
  6.4 7.4 %all-to-all-start = ((s32[16,1,64]{2,1,0:T(1,128)}), s32[16,1,64]{2,1,0:T(1,128)S(1)}, u32[]{:S(2)}, u32[]{:S(2)}) async-start(s32[16,1,64]{2,1,0:T(1,128)} %all_to_all.11), calls=%async_computation | async-start | bytes 16384 | tf_op jit(solution)/shard_map/all_to_all | solution.py:84
  13.8 1.8 %fusion.75 = (f32[256]{0:T(256)S(1)}, f32[256,512]{1,0:T(8,128)S(1)}) fusion(bf16[512,512]{1,0:T(8,128)(2,1)} %param.31, bf16[256,227]{0,1:T(8,128)(2,1)} %param.22, bf16[227,512]{1,0:T(8,128)(2,1)} %param.30), kind=kOutput, calls=%fused_computation.108 | convolution fusion | flops 194510592 | bytes 1398272 | tf_op jit(solution)/shard_map/dot_general | solution.py:15
  16.5 3.5 %scatter_custom_fusion.1 = bf16[1024,512]{1,0:T(8,128)(2,1)} fusion(s32[512]{0:T(512)S(1)} %bitcast.56, bf16[512,512]{1,0:T(8,128)(2,1)S(1)} %reshape.277, bf16[]{:T(256)} %constant.30.clone.1), kind=kCustom, calls=%fused_computation.41 | custom fusion | bytes 1048578 | tf_op jit(solution)/shard_map/scatter | solution.py:70
  20.1 6.0 %all-to-all-start.1 = ((bf16[16,64,512]{2,1,0:T(8,128)(2,1)}), bf16[16,64,512]{2,1,0:T(8,128)(2,1)}, u32[]{:S(2)}, u32[]{:S(2)}) async-start(bf16[16,64,512]{2,1,0:T(8,128)(2,1)} %bitcast.2), calls=%async_computation.1 | async-start | bytes 2097152 | tf_op jit(solution)/shard_map/all_to_all | solution.py:83
  27.0 0.4 broadcast_in_dim.14
  27.4 1.7 %reshape.238 = f32[768,512]{1,0:T(8,128)} reshape(f32[256,3,512]{2,1,0:T(4,128)S(1)} %broadcast_in_dim.14) | data formatting | bytes 3145728 | tf_op jit(solution)/shard_map/reshape | solution.py:119
  29.1 1.2 %fusion.25 = f32[32,512]{1,0:T(8,128)S(1)} fusion(bf16[32,512]{1,0:T(8,128)(2,1)S(1)} %copy-done.5, bf16[1024,512]{1,0:T(8,128)(2,1)} %param.32), kind=kOutput, calls=%fused_computation.38 | convolution fusion | flops 16777216 | bytes 622592 | tf_op jit(solution)/shard_map/dot_general | solution.py:79
  30.5 0.5 broadcast.246
  31.0 0.7 reduce.8
  31.8 4.9 %gather_fusion = f32[1024,512]{1,0:T(8,128)} fusion(f32[33,512]{1,0:T(8,128)S(1)} %concatenate.12, s32[1024]{0:T(1024)S(1)} %broadcast_clamp_fusion), kind=kCustom, calls=%fused_computation | custom fusion | bytes 4198400 | tf_op jit(solution)/shard_map/gather | solution.py:88
  36.6 12.5 %all-to-all-done.1 = bf16[16,64,512]{2,1,0:T(8,128)(2,1)} async-done(((bf16[16,64,512]{2,1,0:T(8,128)(2,1)}), bf16[16,64,512]{2,1,0:T(8,128)(2,1)}, u32[]{:S(2)}, u32[]{:S(2)}) %all-to-all-start.1) | async-done | bytes 1048608 | tf_op jit(solution)/shard_map/all_to_all | solution.py:83
  49.1 3.6 %fusion.76 = (f32[16,64]{1,0:T(8,128)S(1)}, f32[16,64,512]{2,1,0:T(8,128)S(1)}) fusion(bf16[512,512]{1,0:T(8,128)(2,1)} %param.33, f32[16,64,512]{2,1,0:T(8,128)} %bitcast.51, bf16[16,64,512]{2,1,0:T(8,128)(2,1)} %all-to-all-done.1, bf16[1024,512]{1,0:T(8,128)(2,1)} %param.32), kind=kOutput, calls=%fused_computation.109 | convolution fusion | flops 1077410816 | bytes 6295552 | tf_op jit(solution)/shard_map/pch,hk->pck/dot_general | solution.py:90
  52.8 0.4 multiply_reduce_fusion
  53.2 0.3 multiply_convert_fusion
  53.6 0.5 convolution_convert_fusion.1
  54.0 1.9 %fusion.79 = (f32[32]{0:T(128)S(1)}, f32[32,512]{1,0:T(8,128)S(1)}) fusion(bf16[512,512]{1,0:T(8,128)(2,1)} %param.35, bf16[1024,512]{1,0:T(8,128)(2,1)} %param.34, bf16[32,512]{1,0:T(8,128)(2,1)S(1)} %convolution_convert_fusion.1, bf16[32,512]{1,0:T(8,128)(2,1)S(1)} %copy-done.5), kind=kOutput, calls=%fused_computation.110 | convolution fusion | flops 50560992 | bytes 1704064 | tf_op jit(solution)/shard_map/dot_general | solution.py:15
  56.3 24.1 %all_gather.6 = bf16[512,512]{1,0:T(8,128)(2,1)S(1)} all-gather(bf16[32,512]{1,0:T(8,128)(2,1)S(1)} %add_convert_fusion.1), channel_id=1, replica_groups=mesh['groups'=2,'lat'=16] {'lat'}, dimensions={0}, use_global_device_ids=true | all-gather | bytes 557056 | tf_op jit(solution)/shard_map/all_gather | solution.py:102
  80.6 1.2 %gather_fusion.1 = bf16[256,512]{1,0:T(8,128)(2,1)S(1)} fusion(bf16[512,512]{1,0:T(8,128)(2,1)S(1)} %all_gather.6, s32[1024]{0:T(1024)S(1)} %pad_clamp_fusion.1), kind=kCustom, calls=%fused_computation.1 | custom fusion | bytes 525312 | tf_op jit(solution)/shard_map/gather | solution.py:103
  81.8 2.0 %fusion.82 = (f32[256]{0:T(256)S(1)}, f32[256,512]{1,0:T(8,128)S(1)}) fusion(bf16[512,512]{1,0:T(8,128)(2,1)} %param.37, bf16[256,512]{1,0:T(8,128)(2,1)S(1)} %gather_fusion.1, bf16[1024,512]{1,0:T(8,128)(2,1)} %param.36, f32[32,512]{1,0:T(8,128)S(1)} %fusion.21), kind=kOutput, calls=%fused_computation.111 | convolution fusion | flops 269352704 | bytes 1901568 | tf_op jit(solution)/shard_map/dot_general | solution.py:15
  84.2 0.6 fusion.85
  85.1 19.1 %all_gather.7 = bf16[512,512]{1,0:T(8,128)(2,1)S(1)} all-gather(bf16[32,512]{1,0:T(8,128)(2,1)S(1)} %add_convert_fusion), channel_id=1, replica_groups=mesh['groups'=2,'lat'=16] {'lat'}, dimensions={0}, use_global_device_ids=true | all-gather | bytes 557056 | tf_op jit(solution)/shard_map/all_gather | solution.py:115
  104.2 2.7 %gather_fusion.2 = bf16[768,512]{1,0:T(8,128)(2,1)S(1)} fusion(bf16[512,512]{1,0:T(8,128)(2,1)S(1)} %all_gather.7, s32[1024]{0:T(1024)S(1)} %pad_clamp_fusion), kind=kCustom, calls=%fused_computation.2 | custom fusion | bytes 1575936 | tf_op jit(solution)/shard_map/gather | solution.py:116
  106.9 2.9 %fusion.88 = (f32[768]{0:T(1024)S(1)}, f32[768,512]{1,0:T(8,128)S(1)}) fusion(bf16[512,512]{1,0:T(8,128)(2,1)} %param.41, f32[768,512]{1,0:T(8,128)} %reshape.238, bf16[768,512]{1,0:T(8,128)(2,1)S(1)} %gather_fusion.2, bf16[1024,512]{1,0:T(8,128)(2,1)} %param.40), kind=kOutput, calls=%fused_computation.113 | convolution fusion | flops 808058112 | bytes 4983808 | tf_op jit(solution)/shard_map/dot_general | solution.py:15
  109.8 0.3 multiply_reduce_fusion.1
  110.4 0.5 reshape.239
  110.9 1.4 %reduce.1 = bf16[256,512]{1,0:T(8,128)(2,1)S(1)} reduce(bf16[256,3,512]{2,1,0:T(4,128)(2,1)S(1)} %reshape.239, bf16[]{:T(256)} %constant.30.clone.1), dimensions={1}, to_apply=%region_16.17.clone | reduce | flops 262144 | bytes 1048578 | tf_op jit(solution)/shard_map/reduce_sum | solution.py:121
  112.3 2.3 %convolution_convert_fusion = bf16[256,227]{0,1:T(8,128)(2,1)} fusion(bf16[512,227]{0,1:T(8,128)(2,1)} %param.43, bf16[1024,512]{1,0:T(8,128)(2,1)S(1)} %copy-done, bf16[256,512]{1,0:T(8,128)(2,1)S(1)} %reduce.1, bf16[256,512]{1,0:T(8,128)(2,1)S(1)} %copy-done.2), kind=kOutput, calls=%fused_computation.14 | convolution fusion | flops 329704192 | bytes 1921536 | tf_op jit(solution)/shard_map/dot_general | solution.py:128
  (71 shorter events, 4.3 us)
Async XLA Ops:
  0.0 112.3 %copy-start = (bf16[1024,512]{1,0:T(8,128)(2,1)S(1)}, bf16[1024,512]{1,0:T(8,128)(2,1)}, u32[]{:S(2)}) copy-start(bf16[1024,512]{1,0:T(8,128)(2,1)} %param.42) | copy-start | bytes 3145732
  6.4 13.7 %all-to-all-start = ((s32[16,1,64]{2,1,0:T(1,128)}), s32[16,1,64]{2,1,0:T(1,128)S(1)}, u32[]{:S(2)}, u32[]{:S(2)}) async-start(s32[16,1,64]{2,1,0:T(1,128)} %all_to_all.11), calls=%async_computation | async-start | bytes 16384 | tf_op jit(solution)/shard_map/all_to_all | solution.py:84
  16.0 10.7 %copy-start.1 = (bf16[256,512]{1,0:T(8,128)(2,1)}, bf16[256,512]{1,0:T(8,128)(2,1)S(1)}, u32[]{:S(2)}) copy-start(bf16[256,512]{1,0:T(8,128)(2,1)S(1)} %multiply_convert_fusion.7) | copy-start | bytes 786436
  16.3 9.9 %copy-start.8 = (s32[32,8]{0,1:T(8,128)S(1)}, s32[32,8]{0,1:T(8,128)}, u32[]{:S(2)}) copy-start(s32[32,8]{0,1:T(8,128)} %param.27) | copy-start | bytes 3076
  16.3 9.9 %copy-start.9 = (s32[32,8]{0,1:T(8,128)S(1)}, s32[32,8]{0,1:T(8,128)}, u32[]{:S(2)}) copy-start(s32[32,8]{0,1:T(8,128)} %param.26) | copy-start | bytes 3076
  16.3 10.0 %copy-start.10 = (s32[256,3]{0,1:T(4,128)S(1)}, s32[256,3]{0,1:T(4,128)}, u32[]{:S(2)}) copy-start(s32[256,3]{0,1:T(4,128)} %param.29) | copy-start | bytes 9220
  16.3 10.0 %copy-start.11 = (s32[256,3]{0,1:T(4,128)S(1)}, s32[256,3]{0,1:T(4,128)}, u32[]{:S(2)}) copy-start(s32[256,3]{0,1:T(4,128)} %param.28) | copy-start | bytes 9220
  16.3 10.4 %copy-start.7 = (bf16[1024,512]{1,0:T(8,128)(2,1)S(1)}, bf16[1024,512]{1,0:T(8,128)(2,1)}, u32[]{:S(2)}) copy-start(bf16[1024,512]{1,0:T(8,128)(2,1)} %param.40) | copy-start | bytes 3145732
  20.1 29.0 %all-to-all-start.1 = ((bf16[16,64,512]{2,1,0:T(8,128)(2,1)}), bf16[16,64,512]{2,1,0:T(8,128)(2,1)}, u32[]{:S(2)}, u32[]{:S(2)}) async-start(bf16[16,64,512]{2,1,0:T(8,128)(2,1)} %bitcast.2), calls=%async_computation.1 | async-start | bytes 2097152 | tf_op jit(solution)/shard_map/all_to_all | solution.py:83
  27.4 1.7 %copy-start.5 = (bf16[32,512]{1,0:T(8,128)(2,1)S(1)}, bf16[32,512]{1,0:T(8,128)(2,1)}, u32[]{:S(2)}) copy-start(bf16[32,512]{1,0:T(8,128)(2,1)} %param.23) | copy-start | bytes 98308
  53.6 26.8 %copy-start.6 = (bf16[1024,512]{1,0:T(8,128)(2,1)S(1)}, bf16[1024,512]{1,0:T(8,128)(2,1)}, u32[]{:S(2)}) copy-start(bf16[1024,512]{1,0:T(8,128)(2,1)} %param.36) | copy-start | bytes 3145732
  81.7 2.5 %copy-start.3 = (bf16[1024,512]{1,0:T(8,128)(2,1)S(1)}, bf16[1024,512]{1,0:T(8,128)(2,1)}, u32[]{:S(2)}) copy-start(bf16[1024,512]{1,0:T(8,128)(2,1)} %param.38) | copy-start | bytes 3145732
  81.7 2.5 %copy-start.4 = (bf16[512,512]{1,0:T(8,128)(2,1)S(1)}, bf16[512,512]{1,0:T(8,128)(2,1)}, u32[]{:S(2)}) copy-start(bf16[512,512]{1,0:T(8,128)(2,1)} %param.39) | copy-start | bytes 1572868
  110.4 1.9 %copy-start.2 = (bf16[256,512]{1,0:T(8,128)(2,1)S(1)}, bf16[256,512]{1,0:T(8,128)(2,1)}, u32[]{:S(2)}) copy-start(bf16[256,512]{1,0:T(8,128)(2,1)} %copy-done.1) | copy-start | bytes 786436
where the time goes:
time: 115 us
  blocking collectives  43.2 us (38%)
  local copies, waits for them, and re-layouts  21.9 us (19%)
  matrix products  17.3 us (15%)
  starting transfers between devices  13.4 us (12%)
  waiting for transfers between devices  12.5 us (11%)
  other arithmetic  5.82 us (5%)
    all_gather x1, blocking collectives, body(): every_mesh = lax.all_gather(mesh_latent, 'lat', axis=0, tiled=True)  24.1 us
    all_gather x1, blocking collectives, body(): every_final = lax.all_gather(mesh_final, 'lat', axis=0, tiled=True)  19.1 us
    all_to_all x1, waiting for transfers between devices, body(): lax.all_to_all(send_rows, 'lat', split_axis=0, concat_axis=0, tiled=True)  12.5 us
    dot_general x5, matrix products, mlp_tail(): jnp.dot(hidden, w_out, preferred_element_type=jnp.float32)  9.18 us
    all_to_all x1, starting transfers between devices, body(): lax.all_to_all(send_nodes, 'lat', split_axis=0, concat_axis=0, tiled=True)  7.36 us
    all_to_all x1, starting transfers between devices, body(): lax.all_to_all(send_rows, 'lat', split_axis=0, concat_axis=0, tiled=True)  6.02 us
    gather x1, local copies, waits for them, and re-layouts, body(): preact = preact + receiver_padded[slot_nodes]  4.88 us
    dot_general x1, matrix products, body(): jnp.einsum('pch,hk->pck', hidden, g2m_out, preferred_element_type=jnp.flo...  3.63 us
  transfers between devices with their start and end apart: 2, of which 1 were waited for; matrix products, arithmetic and copies ran while one was open for 14% of the time, Pallas kernels for 0%

commit v1 on v0

--- a/solution.py
+++ b/solution.py
@@ -1,7 +1,14 @@
+import functools
+
 import jax
 import jax.numpy as jnp
 from jax import lax
+from jax.experimental import pallas as pl
+from jax.experimental.pallas import tpu as pltpu
 from jax.sharding import PartitionSpec as P
+
+BF16 = jnp.bfloat16
+F32 = jnp.float32
 
 
 def layer_norm(values):
@@ -128,7 +135,307 @@
     return jnp.dot(grid_hidden, grid_out, preferred_element_type=jnp.float32).astype(jnp.bfloat16)
 
 
+def dot(a, b):
+    return jnp.dot(a, b, preferred_element_type=F32)
+
+
+def dot_lhs_t(a, b):
+    return lax.dot_general(a, b, (((0,), (0,)), ((), ())), preferred_element_type=F32)
+
+
+def dot_rhs_t(a, b):
+    return lax.dot_general(a, b, (((1,), (1,)), ((), ())), preferred_element_type=F32)
+
+
+def silu(v):
+    half = 0.5 * v
+    return half + half * jnp.tanh(half)
+
+
+def tail(preact, w_out):
+    return layer_norm(dot(silu(preact).astype(BF16), w_out))
+
+
+WEIGHTS = 13
+
+
+def fused(depth, *refs):
+    state, embed, g2m_o, g2m_n, mm_o, mm_n, m2g_o, m2g_n, grid_out = refs[:9]
+    hbm = refs[9 : 9 + WEIGHTS]
+    out = refs[9 + WEIGHTS]
+    scratch = refs[10 + WEIGHTS :]
+    vmem = scratch[:WEIGHTS]
+    (buf1, buf2, buf3, part, got1, sum2, got2, sum3, got3, down_recv, grid_part, state_pad, embed_pad) = scratch[
+        WEIGHTS : WEIGHTS + 13
+    ]
+    (load_sem, send1, recv1, send2, recv2, send3, recv3, cs, cr, xs, xr, zs, zr) = scratch[
+        WEIGHTS + 13 :
+    ]
+    me = lax.axis_index("lat")
+    z, x, c = me // 4, (me // 2) % 2, me % 2
+    rows, width = embed.shape
+    channels = state.shape[0]
+    count = 4 * depth
+
+    def at(zz, xx, cc):
+        return (zz * 2 + xx) * 2 + cc
+
+    def block(zz, xx, cc):
+        return (cc * 2 + xx) * depth + zz
+
+    def away(d):
+        return (z + d) % depth
+
+    def put(src, dst, send, recv, target):
+        return pltpu.make_async_remote_copy(
+            src_ref=src,
+            dst_ref=dst,
+            send_sem=send,
+            recv_sem=recv,
+            device_id={"lat": target},
+            device_id_type=pl.DeviceIdType.MESH,
+        )
+
+    loads = [pltpu.make_async_copy(h, v, load_sem.at[i]) for i, (h, v) in enumerate(zip(hbm, vmem))]
+    (embed_in, embed_out, g2m_in, g2m_out, mesh_in, mesh_out, edge_in, edge_out, node_in, node_out, m2g_in, m2g_out, grid_in) = vmem
+    barrier = pltpu.get_barrier_semaphore()
+    partners = [at(away(d), x, c) for d in range(1, depth)] + [at(z, 1 - x, c), at(z, x, 1 - c)]
+    for partner in partners:
+        pl.semaphore_signal(
+            barrier, inc=1, device_id={"lat": partner}, device_id_type=pl.DeviceIdType.MESH
+        )
+    for load in loads:
+        load.start()
+
+    class Gather:
+        def __init__(self, buf, send, recv):
+            self.buf, self.send, self.recv, self.sent = buf, send, recv, []
+
+        def copy(self, q, target):
+            n = len(self.sent)
+            made = put(self.buf.at[q], self.buf.at[q], self.send.at[n], self.recv.at[q], target)
+            made.start()
+            self.sent.append(made)
+
+        def arrive(self, q):
+            put(self.buf.at[q], self.buf.at[q], self.send.at[0], self.recv.at[q], me).wait_recv()
+
+        def begin(self, values):
+            own = block(z, x, c)
+            self.buf[own] = values
+            self.copy(own, at(z, 1 - x, c))
+            for d in range(1, depth):
+                self.copy(own, at(away(d), x, c))
+            self.copy(own, at(z, x, 1 - c))
+
+        def forward(self):
+            for d in range(1, depth):
+                q = block(away(d), x, c)
+                self.arrive(q)
+                self.copy(q, at(z, 1 - x, c))
+                self.copy(q, at(z, x, 1 - c))
+
+        def cross(self):
+            for d in range(depth):
+                q = block(away(d), 1 - x, c)
+                self.arrive(q)
+                self.copy(q, at(z, x, 1 - c))
+
+        def finish(self):
+            for xx in (x, 1 - x):
+                for d in range(depth):
+                    self.arrive(block(away(d), xx, 1 - c))
+
+        def rows(self):
+            return self.buf[...].reshape(count * rows, width)
+
+        def drain(self):
+            for made in self.sent:
+                made.wait_send()
+
+    def place(owner, node):
+        return (((owner & 1) * 2 + ((owner >> 1) & 1)) * depth + (owner >> 2)) * rows + node
+
+    def picks(column):
+        lanes = lax.broadcasted_iota(jnp.int32, (column.shape[0], count * rows), 1)
+        return (lanes == column).astype(F32).astype(BF16)
+
+    g2m_at = place(g2m_o[...], g2m_n[...])
+    g2m_t = jnp.transpose(g2m_at)
+    fan_grid = g2m_at.shape[0]
+
+    own_rows = embed[...]
+    first = Gather(buf1, send1, recv1)
+    pl.semaphore_wait(barrier, len(partners))
+    first.begin(own_rows)
+
+    loads[0].wait()
+    loads[1].wait()
+    whole = channels // 16 * 16
+    for padded, source in ((state_pad, state), (embed_pad, embed_in)):
+        padded[whole:] = jnp.zeros((padded.shape[0] - whole, padded.shape[1]), BF16)
+        padded[:channels] = source[...]
+    latent = tail(dot_lhs_t(state_pad[...], embed_pad[...]), embed_out[...]).astype(BF16)
+    first.forward()
+    loads[2].wait()
+    sender = dot(latent, g2m_in[:width])
+    first.cross()
+    loads[3].wait()
+    loads[4].wait()
+    mesh_part = dot(own_rows, mesh_in[:width])
+    first.finish()
+    every = first.rows()
+    messages = []
+    for k in range(fan_grid):
+        picked = dot(picks(g2m_t[:, k : k + 1]), every).astype(BF16)
+        messages.append(tail(sender + dot(picked, g2m_in[width:]), g2m_out[...]).astype(BF16))
+
+    def partial(xx, cc):
+        span = depth * rows
+        places = lax.broadcasted_iota(jnp.int32, (span, g2m_at.shape[1]), 0) + (cc * 2 + xx) * span
+        total = jnp.zeros((span, width), F32)
+        for k in range(fan_grid):
+            hits = (places == g2m_at[k : k + 1, :]).astype(F32).astype(BF16)
+            total = total + dot(hits, messages[k])
+        return total.reshape(depth, rows, width)
+
+    def group(xx, cc):
+        return pl.ds((cc * 2 + xx) * depth, depth)
+
+    sends = []
+    for n, xx in enumerate((1 - x, x)):
+        part[group(xx, 1 - c)] = partial(xx, 1 - c).astype(BF16)
+        made = put(
+            part.at[group(xx, 1 - c)],
+            got1.at[n],
+            cs.at[n],
+            cr.at[n],
+            at(z, x, 1 - c),
+        )
+        made.start()
+        sends.append(made)
+    cross_part = partial(1 - x, c)
+    part[group(x, c)] = partial(x, c).astype(BF16)
+    sends[0].wait_recv()
+    sum2[...] = (cross_part + got1[0].astype(F32)).astype(BF16)
+    for d in list(range(1, depth)) + [0]:
+        zz = away(d)
+        made = put(sum2.at[zz], got2.at[zz], xs.at[zz], xr.at[zz], at(z, 1 - x, c))
+        made.start()
+        sends.append(made)
+    sends[1].wait_recv()
+
+    def ready(zz):
+        put(sum2.at[zz], got2.at[zz], xs.at[zz], xr.at[zz], at(z, 1 - x, c)).wait_recv()
+        return (
+            part[block(zz, x, c)].astype(F32) + got1[1, zz].astype(F32) + got2[zz].astype(F32)
+        )
+
+    for d in range(1, depth):
+        zz = away(d)
+        sum3[zz] = ready(zz).astype(BF16)
+        made = put(sum3.at[zz], got3.at[z], zs.at[zz], zr.at[z], at(zz, x, c))
+        made.start()
+        sends.append(made)
+    g2m_sum = ready(z)
+    for d in range(1, depth):
+        zz = away(d)
+        put(sum3.at[zz], got3.at[zz], zs.at[zz], zr.at[zz], at(zz, x, c)).wait_recv()
+        g2m_sum = g2m_sum + got3[zz].astype(F32)
+    loads[5].wait()
+    mesh_latent = (
+        own_rows.astype(F32)
+        + tail(mesh_part + dot(g2m_sum.astype(BF16), mesh_in[width:]), mesh_out[...])
+    ).astype(BF16)
+
+    second = Gather(buf2, send2, recv2)
+    second.begin(mesh_latent)
+    loads[6].wait()
+    loads[8].wait()
+    receiver = dot(mesh_latent, edge_in[width:])
+    node_part = dot(mesh_latent, node_in[:width])
+    second.forward()
+    loads[10].wait()
+    down_recv[...] = dot(latent, m2g_in[width:])
+    second.cross()
+    loads[12].wait()
+    grid_part[...] = dot(latent, grid_in[:width])
+    mm_t = jnp.transpose(place(mm_o[...], mm_n[...]))
+    fan_mesh = mm_t.shape[1]
+    mm_picks = jnp.concatenate([picks(mm_t[:, k : k + 1]) for k in range(fan_mesh)], axis=0)
+    loads[7].wait()
+    second.finish()
+    picked = dot(mm_picks, second.rows()).astype(BF16)
+    preact = receiver[None] + dot(picked, edge_in[:width]).reshape(fan_mesh, rows, width)
+    message = tail(preact.reshape(fan_mesh * rows, width), edge_out[...]).astype(BF16)
+    mesh_sum = jnp.sum(message.astype(F32).reshape(fan_mesh, rows, width), axis=0)
+    loads[9].wait()
+    mesh_final = (
+        mesh_latent.astype(F32)
+        + tail(node_part + dot(mesh_sum.astype(BF16), node_in[width:]), node_out[...])
+    ).astype(BF16)
+
+    third = Gather(buf3, send3, recv3)
+    third.begin(mesh_final)
+    m2g_t = jnp.transpose(place(m2g_o[...], m2g_n[...]))
+    fan_down = m2g_t.shape[1]
+    loads[11].wait()
+    third.forward()
+    third.cross()
+    third.finish()
+    every = third.rows()
+    down_sum = None
+    for k in range(fan_down):
+        picked = dot(picks(m2g_t[:, k : k + 1]), every).astype(BF16)
+        message = tail(down_recv[...] + dot(picked, m2g_in[:width]), m2g_out[...])
+        message = message.astype(BF16).astype(F32)
+        down_sum = message if down_sum is None else down_sum + message
+    hidden = silu(grid_part[...] + dot(down_sum.astype(BF16), grid_in[width:])).astype(BF16)
+    out[...] = dot_rhs_t(grid_out[...], hidden).astype(BF16)
+    for made in sends:
+        made.wait_send()
+    for gather in (first, second, third):
+        gather.drain()
+
+
+def fused_body(*args):
+    state, embed, *rest = args
+    indices, weights = rest[:6], rest[6:]
+    lat = lax.axis_size("lat")
+    depth = lat // 4
+    rows, width = embed.shape
+    grid_rows, channels = state.shape
+    vmem_spec = pl.BlockSpec(memory_space=pltpu.VMEM)
+    hbm_spec = pl.BlockSpec(memory_space=pltpu.HBM)
+    channel_pad = -(-channels // 128) * 128
+    dma = pltpu.SemaphoreType.DMA
+    gather_sems = [dma((4 * depth,)), dma((lat,))]
+    result = pl.pallas_call(
+        functools.partial(fused, depth),
+        out_shape=jax.ShapeDtypeStruct((channels, grid_rows), BF16),
+        in_specs=[vmem_spec] * 9 + [hbm_spec] * WEIGHTS,
+        out_specs=vmem_spec,
+        scratch_shapes=[pltpu.VMEM(w.shape, w.dtype) for w in weights[:WEIGHTS]]
+        + [pltpu.VMEM((lat, rows, width), BF16)] * 4
+        + [pltpu.VMEM((2, depth, rows, width), BF16)]
+        + [pltpu.VMEM((depth, rows, width), BF16)] * 4
+        + [pltpu.VMEM((grid_rows, width), F32)] * 2
+        + [pltpu.VMEM((channel_pad, grid_rows), BF16), pltpu.VMEM((channel_pad, width), BF16)]
+        + [dma((WEIGHTS,))]
+        + gather_sems * 3
+        + [dma((2,))] * 2
+        + [dma((depth,))] * 4,
+        compiler_params=pltpu.CompilerParams(
+            collective_id=0, has_side_effects=True, vmem_limit_bytes=63 * 1024 * 1024
+        ),
+        cost_estimate=pl.CostEstimate(flops=2 * 10**9, bytes_accessed=10**7, transcendentals=10**6),
+    )(state.T, embed, *[i.T for i in indices], weights[WEIGHTS].T, *weights[:WEIGHTS])
+    return result.T
+
+
 def solution(mesh):
+    lat = mesh.shape["lat"]
+    step = fused_body if lat % 4 == 0 and 8 <= lat <= 32 else body
     in_specs = (
         P(("groups", "lat"), None),
         P(("groups", "lat"), None),
@@ -154,4 +461,4 @@
         P(),
     )
     out_specs = P(("groups", "lat"), None)
-    return jax.shard_map(body, mesh=mesh, in_specs=in_specs, out_specs=out_specs, check_vma=False)
+    return jax.shard_map(step, mesh=mesh, in_specs=in_specs, out_specs=out_specs, check_vma=False)

time: 115 us -> 49.9 us (0.43)
  Pallas kernels: 0 us -> 47.7 us
  blocking collectives: 43.2 us -> 0 us
  local copies, waits for them, and re-layouts: 21.9 us -> 1.56 us
  matrix products: 17.3 us -> 0 us
  starting transfers between devices: 13.4 us -> 0 us
  waiting for transfers between devices: 12.5 us -> 0 us
  other arithmetic: 5.82 us -> 0 us
    pallas_call x0 -> x1, Pallas kernels: none -> 47.7 us  [fused_body(): pl.pallas_call(functools.partial(fused, depth), out_shape=jax.ShapeDtypeS...]
    all_gather x2 -> x0, blocking collectives: 43.2 us -> none  [the longest x1 24.1 us: body(): every_mesh = lax.all_gather(mesh_latent, 'lat', axis=0, tiled=True)]
    dot_general x11 -> x0, matrix products: 17.3 us -> none  [the longest x5 9.18 us: mlp_tail(): jnp.dot(hidden, w_out, preferred_element_type=jnp.float32)]
    all_to_all x2 -> x0, starting transfers between devices: 13.4 us -> none  [the longest x1 7.36 us: body(): lax.all_to_all(send_nodes, 'lat', split_axis=0, concat_axis=0, tiled=True)]
    all_to_all x2 -> x0, waiting for transfers between devices: 12.5 us -> none  [the longest x1 12.5 us: body(): lax.all_to_all(send_rows, 'lat', split_axis=0, concat_axis=0, tiled=True)]
    gather x3 -> x0, local copies, waits for them, and re-layouts: 8.73 us -> none  [the longest x1 4.88 us: body(): preact = preact + receiver_padded[slot_nodes]]
    scatter x2 -> x0, local copies, waits for them, and re-layouts: 5.96 us -> none  [the longest x1 3.52 us: body(): jnp.zeros((peer_count * cap_grid, latent_width), jnp.bfloat16)]
    reduce_sum x9 -> x0, other arithmetic: 3.4 us -> none  [the longest x6 1.51 us: layer_norm(): spread = jnp.mean(center * center, axis=-1, keepdims=True)]
  transfers between devices with their start and end apart: 2 -> 0, of which waited for: 1 -> 0; matrix products, arithmetic and copies ran while one was open for 14% -> 0% of each run, Pallas kernels for 0% -> 0%
where the time goes in v1:
time: 49.9 us; the launch traced here: 49.3 us
  Pallas kernels  47.7 us (96%)
  local copies, waits for them, and re-layouts  1.56 us (3%)
    pallas_call x1, Pallas kernels, fused_body(): pl.pallas_call(functools.partial(fused, depth), out_shape=jax.ShapeDtypeS...  47.7 us
    unnamed x1, local copies, waits for them, and re-layouts  1.56 us

profile of v1, /device:TPU:0, one launch (start us, length us, event | category | flops | bytes accessed | tf_op | source)
XLA Modules:
  0.0 49.3 jit_solution(15276337327914926224)
XLA Ops:
  0.0 47.7 %shard_map.208 = bf16[227,256]{1,0:T(8,128)(2,1)} custom-call(bf16[227,256]{1,0:T(8,128)(2,1)} %bitcast.11, bf16[32,512]{1,0:T(8,128)(2,1)} %refs_1_.1, s32[2,256]{1,0:T(2,128)} %bitcast.16, s32[2,256]{1,0:T(2,128)} %bitcast.17, s32[8,32]{1,0:T(8,128)} %bitcast.12, s32[8,32]{1,0:T(8,128)} %bitcast.13, s32[3,256]{1,0:T(4,128)} %bitcast.14, ...), custom_call_target="tpu_custom_call" | custom-call | flops 2000000000 | bytes 10000000 | tf_op jit(solution)/shard_map/pallas_call | solution.py:413
  47.7 1.6 %copy.24 = bf16[256,227]{0,1:T(8,128)(2,1)} copy(bf16[256,227]{0,1:T(8,128)(2,1)} %bitcast.9) | data formatting | bytes 232448

commit v2 on v1

--- a/solution.py
+++ b/solution.py
@@ -199,7 +199,7 @@
     loads = [pltpu.make_async_copy(h, v, load_sem.at[i]) for i, (h, v) in enumerate(zip(hbm, vmem))]
     (embed_in, embed_out, g2m_in, g2m_out, mesh_in, mesh_out, edge_in, edge_out, node_in, node_out, m2g_in, m2g_out, grid_in) = vmem
     barrier = pltpu.get_barrier_semaphore()
-    partners = [at(away(d), x, c) for d in range(1, depth)] + [at(z, 1 - x, c), at(z, x, 1 - c)]
+    partners = [at(away(d), xx, c) for d in range(1, depth) for xx in (x, 1 - x)] + [at(z, 1 - x, c), at(z, x, 1 - c)]
     for partner in partners:
         pl.semaphore_signal(
             barrier, inc=1, device_id={"lat": partner}, device_id_type=pl.DeviceIdType.MESH
@@ -223,23 +223,23 @@
         def begin(self, values):
             own = block(z, x, c)
             self.buf[own] = values
+            for d in range(1, depth):
+                self.copy(own, at(away(d), 1 - x, c))
+                self.copy(own, at(away(d), x, c))
             self.copy(own, at(z, 1 - x, c))
+            self.copy(own, at(z, x, 1 - c))
+
+        def forward(self):
+            q = block(z, 1 - x, c)
+            self.arrive(q)
+            self.copy(q, at(z, x, 1 - c))
+
+        def cross(self):
             for d in range(1, depth):
-                self.copy(own, at(away(d), x, c))
-            self.copy(own, at(z, x, 1 - c))
-
-        def forward(self):
-            for d in range(1, depth):
-                q = block(away(d), x, c)
-                self.arrive(q)
-                self.copy(q, at(z, 1 - x, c))
-                self.copy(q, at(z, x, 1 - c))
-
-        def cross(self):
-            for d in range(depth):
-                q = block(away(d), 1 - x, c)
-                self.arrive(q)
-                self.copy(q, at(z, x, 1 - c))
+                for xx in (x, 1 - x):
+                    q = block(away(d), xx, c)
+                    self.arrive(q)
+                    self.copy(q, at(z, x, 1 - c))
 
         def finish(self):
             for xx in (x, 1 - x):

time: 49.9 us -> 46.8 us (0.938); the launches traced: 49.3 us -> 46.7 us
  Pallas kernels: 47.7 us -> 45.1 us
    pallas_call x1, Pallas kernels: 47.7 us -> 45.1 us  [fused_body(): pl.pallas_call(functools.partial(fused, depth), out_shape=jax.ShapeDtypeS...]
where the time goes in v2:
time: 46.8 us; the launch traced here: 46.7 us
  Pallas kernels  45.1 us (96%)
  local copies, waits for them, and re-layouts  1.56 us (3%)
    pallas_call x1, Pallas kernels, fused_body(): pl.pallas_call(functools.partial(fused, depth), out_shape=jax.ShapeDtypeS...  45.1 us
    unnamed x1, local copies, waits for them, and re-layouts  1.56 us

profile of v2, /device:TPU:0, one launch (start us, length us, event | category | flops | bytes accessed | tf_op | source)
XLA Modules:
  0.0 46.7 jit_solution(10621443475650066017)
XLA Ops:
  0.0 45.1 %shard_map.208 = bf16[227,256]{1,0:T(8,128)(2,1)} custom-call(bf16[227,256]{1,0:T(8,128)(2,1)} %bitcast.11, bf16[32,512]{1,0:T(8,128)(2,1)} %refs_1_.1, s32[2,256]{1,0:T(2,128)} %bitcast.16, s32[2,256]{1,0:T(2,128)} %bitcast.17, s32[8,32]{1,0:T(8,128)} %bitcast.12, s32[8,32]{1,0:T(8,128)} %bitcast.13, s32[3,256]{1,0:T(4,128)} %bitcast.14, ...), custom_call_target="tpu_custom_call" | custom-call | flops 2000000000 | bytes 10000000 | tf_op jit(solution)/shard_map/pallas_call | solution.py:413
  45.1 1.6 %copy.24 = bf16[256,227]{0,1:T(8,128)(2,1)} copy(bf16[256,227]{0,1:T(8,128)(2,1)} %bitcast.9) | data formatting | bytes 232448
